TPU v7x, 256 devices: a whole 4x4x8 slice. The times are simulated.
256 devices in a mesh: pipe: 8 (over z_hi, core), expert: 32 (over z_lo, y, x).
Axes of the slice: x: 4, y: 4, z: 8 (z_hi: 4, z_lo: 2; z = z_hi * 2 + z_lo), core: 2. Of those that a mesh axis runs over, the one named last changes fastest.
Arguments:
- forward_in: bfloat16 [8, 4096, 4096], P('pipe', 'expert'), may hold values from -6 to 6
- forward_route: int32 [8, 4096, 1], P('pipe', 'expert'), may hold values from 0 to 7, as said below
- forward_gate_prob: float32 [8, 4096, 1], P('pipe', 'expert'), may hold values from 0.25 to 1
- backward_in: bfloat16 [8, 4096, 4096], P('pipe', 'expert'), may hold values from -6 to 6
- backward_route: int32 [8, 4096, 1], P('pipe', 'expert'), may hold values from 0 to 7, as said below
- backward_gate_prob: float32 [8, 4096, 1], P('pipe', 'expert'), may hold values from 0.25 to 1
- cotangent: bfloat16 [8, 4096, 4096], P('pipe', 'expert'), may hold values from -6 to 6
- w_gate: bfloat16 [8, 4096, 8192], P('pipe', None, 'expert'), may hold values from -0.09375 to 0.09375
- w_up: bfloat16 [8, 4096, 8192], P('pipe', None, 'expert'), may hold values from -0.09375 to 0.09375
- w_down: bfloat16 [8, 8192, 4096], P('pipe', 'expert'), may hold values from -0.1875 to 0.1875
Outputs:
- next_forward: bfloat16 [8, 4096, 4096], P('pipe', 'expert')
- next_cotangent: bfloat16 [8, 4096, 4096], P('pipe', 'expert')
Inputs may be any that keep to these rules, and one draw needn't show every extreme that they name: `forward_route`: among the 128 tokens of one device at one section no expert is named more than 20 times; in each section one expert is named exactly 20 times by every device's tokens. `backward_route`: among the 128 tokens of one device at one section no expert is named more than 20 times; in each section one expert is named exactly 20 times by every device's tokens.
All inputs are finite; a program needn't handle non-finite values.
Results may differ from a plain program's by a relative error of at most 0.0095.
Values may be sent and summed in bfloat16 or wider, within the bound.
A program may use at most 128 MiB of HBM per device.

v0:
```python
import jax
import jax.numpy as jnp
from jax import lax
from jax.sharding import PartitionSpec as P

GROUP = 4
TOP = 1


def shifted(value, axis, steps):
    count = lax.axis_size(axis)
    pairs = [(source, (source + steps) % count) for source in range(count)]
    return lax.ppermute(value, axis, pairs)


def place_tokens(route, experts, capacity):
    expert_ids = route[:, 0]
    onehot = (expert_ids[:, None] == jnp.arange(experts, dtype=jnp.int32)[None, :]).astype(
        jnp.int32
    )
    before = jnp.cumsum(onehot, axis=0) - onehot
    slot_pos = jnp.sum(onehot * before, axis=1)
    target = expert_ids * capacity + slot_pos
    selector = (jnp.arange(experts * capacity, dtype=jnp.int32)[:, None] == target[None, :]).astype(
        jnp.bfloat16
    )
    return (expert_ids, slot_pos, selector)


def spread_rows(selector, values, experts, capacity):
    width = values.shape[1]
    packed = jnp.dot(selector, values, preferred_element_type=jnp.float32).astype(jnp.bfloat16)
    packed = packed.reshape(experts, 1, capacity, width)
    return jnp.broadcast_to(packed, (experts, GROUP, capacity, width)).reshape(
        experts * GROUP, capacity, width
    )


def contract_last(left, right):
    return lax.dot_general(
        left, right, (((1,), (1,)), ((), ())), preferred_element_type=jnp.float32
    )


def expert_forward(in_rows, w_gate, w_up, w_down):
    sources, items, width = in_rows.shape
    flat_rows = in_rows.reshape(sources * items, width)
    gate_pre = jnp.dot(flat_rows, w_gate, preferred_element_type=jnp.float32)
    up_pre = jnp.dot(flat_rows, w_up, preferred_element_type=jnp.float32)
    hidden = (jax.nn.silu(gate_pre) * up_pre).astype(jnp.bfloat16)
    partial_value = jnp.dot(hidden, w_down, preferred_element_type=jnp.float32)
    return partial_value.astype(jnp.bfloat16).reshape(sources, items, width)


def expert_backward(pair_in, w_gate, w_up, w_down):
    in_rows, grad_rows = pair_in
    sources, items, width = in_rows.shape
    flat_rows = in_rows.reshape(sources * items, width)
    flat_grads = grad_rows.reshape(sources * items, width)
    back_gate = jnp.dot(flat_rows, w_gate, preferred_element_type=jnp.float32)
    back_up = jnp.dot(flat_rows, w_up, preferred_element_type=jnp.float32)
    back_hid = contract_last(flat_grads, w_down)
    sigmoid_g = jax.nn.sigmoid(back_gate)
    grad_gate = (back_hid * back_up * sigmoid_g * (1.0 + back_gate * (1.0 - sigmoid_g))).astype(
        jnp.bfloat16
    )
    grad_up = (back_hid * back_gate * sigmoid_g).astype(jnp.bfloat16)
    partial_value = contract_last(grad_gate, w_gate) + contract_last(grad_up, w_up)
    return partial_value.astype(jnp.bfloat16).reshape(sources, items, width)


def collect_direct(arrived, expert_ids, slot_pos, capacity):
    width = arrived.shape[2]
    flat_rows = arrived.reshape(-1, width)
    member_ids = jnp.arange(GROUP, dtype=jnp.int32)
    where_rows = (expert_ids[:, None] * GROUP + member_ids[None, :]) * capacity + slot_pos[:, None]
    return jnp.sum(flat_rows[where_rows].astype(jnp.float32), axis=1)


def on_device(
    forward_in,
    forward_route,
    forward_gate_prob,
    backward_in,
    backward_route,
    backward_gate_prob,
    cotangent,
    w_gate,
    w_up,
    w_down,
):
    members = lax.axis_size("expert")
    experts = members // GROUP
    fwd_rows = forward_in[0]
    bwd_rows = backward_in[0]
    grad_out = cotangent[0]
    tok_count = fwd_rows.shape[0]
    capacity = (5 * tok_count * TOP // (4 * experts) + 3) // 4 * 4
    gate_w = w_gate[0]
    up_w = w_up[0]
    down_w = w_down[0]
    fwd_ids, fwd_slots, fwd_select = place_tokens(forward_route[0], experts, capacity)
    bwd_ids, bwd_slots, bwd_select = place_tokens(backward_route[0], experts, capacity)
    send_fwd = spread_rows(fwd_select, fwd_rows, experts, capacity)
    send_inputs = spread_rows(bwd_select, bwd_rows, experts, capacity)
    send_grads = spread_rows(bwd_select, grad_out, experts, capacity)
    partial_value = expert_forward(
        lax.all_to_all(send_fwd, "expert", split_axis=0, concat_axis=0, tiled=True),
        gate_w,
        up_w,
        down_w,
    )
    fwd_result = lax.all_to_all(partial_value, "expert", split_axis=0, concat_axis=0, tiled=True)
    partial_value = expert_backward(
        (
            lax.all_to_all(send_inputs, "expert", split_axis=0, concat_axis=0, tiled=True),
            lax.all_to_all(send_grads, "expert", split_axis=0, concat_axis=0, tiled=True),
        ),
        gate_w,
        up_w,
        down_w,
    )
    bwd_result = lax.all_to_all(partial_value, "expert", split_axis=0, concat_axis=0, tiled=True)
    fwd_branch = collect_direct(fwd_result, fwd_ids, fwd_slots, capacity)
    bwd_branch = collect_direct(bwd_result, bwd_ids, bwd_slots, capacity)
    forward_out = (fwd_rows.astype(jnp.float32) + forward_gate_prob[0] * fwd_branch).astype(
        jnp.bfloat16
    )
    backward_out = (grad_out.astype(jnp.float32) + backward_gate_prob[0] * bwd_branch).astype(
        jnp.bfloat16
    )
    next_fwd = shifted(forward_out, "pipe", 1)
    next_grad = shifted(backward_out, "pipe", -1)
    return (next_fwd[None], next_grad[None])


def solution(mesh):
    return jax.shard_map(
        on_device,
        mesh=mesh,
        in_specs=(
            P("pipe", "expert", None),
            P("pipe", "expert", None),
            P("pipe", "expert", None),
            P("pipe", "expert", None),
            P("pipe", "expert", None),
            P("pipe", "expert", None),
            P("pipe", "expert", None),
            P("pipe", None, "expert"),
            P("pipe", None, "expert"),
            P("pipe", "expert", None),
        ),
        out_specs=(P("pipe", "expert", None), P("pipe", "expert", None)),
        check_vma=False,
    )
```

profile of v0, /device:TPU:43, one launch (start us, length us, event | category | flops | bytes accessed | tf_op | source)
XLA Modules:
  0.0 580.3 jit_solution(9820334666749976803)
XLA Ops:
  0.6 0.0 copy-start
  0.6 0.9 fusion.51
  1.5 0.2 reduce_window_sum.17
  1.7 0.8 select_reduce_fusion.1
  2.5 0.7 broadcast_multiply_fusion.1
  3.2 1.7 convolution_convert_fusion.3
  4.9 1.3 broadcast_in_dim.16
  6.3 4.8 broadcast_in_dim.17
  11.1 8.0 %all-to-all-start = ((bf16[32,20,4096]{2,1,0:T(8,128)(2,1)}), bf16[32,20,4096]{2,1,0:T(8,128)(2,1)}, u32[]{:S(2)}, u32[]{:S(2)}) async-start(bf16[32,20,4096]{2,1,0:T(8,128)(2,1)} %bitcast.68), calls=%async_computation | async-start | bytes 12582912 | tf_op jit(solution)/shard_map/all_to_all | solution.py:108
  19.1 0.0 copy-done.6
  19.2 0.1 fusion.50
  19.2 0.2 reduce_window_sum.18
  19.4 0.2 select_reduce_fusion
  19.6 1.7 convolution_convert_fusion.2
  21.3 1.3 broadcast_in_dim.19
  22.7 81.8 %all-to-all-done = bf16[32,20,4096]{2,1,0:T(8,128)(2,1)} async-done(((bf16[32,20,4096]{2,1,0:T(8,128)(2,1)}), bf16[32,20,4096]{2,1,0:T(8,128)(2,1)}, u32[]{:S(2)}, u32[]{:S(2)}) %all-to-all-start) | async-done | bytes 5242912 | tf_op jit(solution)/shard_map/all_to_all | solution.py:108
  104.5 4.8 broadcast_in_dim.20
  109.3 14.4 %all-to-all-start.2 = ((bf16[32,20,4096]{2,1,0:T(8,128)(2,1)}), bf16[32,20,4096]{2,1,0:T(8,128)(2,1)}, u32[]{:S(2)}, u32[]{:S(2)}) async-start(bf16[32,20,4096]{2,1,0:T(8,128)(2,1)} %bitcast.70), calls=%async_computation.2 | async-start | bytes 12582912 | tf_op jit(solution)/shard_map/all_to_all | solution.py:117
  123.7 1.7 convolution_convert_fusion.1
  125.4 1.3 broadcast_in_dim.21
  126.7 75.7 %all-to-all-done.2 = bf16[32,20,4096]{2,1,0:T(8,128)(2,1)} async-done(((bf16[32,20,4096]{2,1,0:T(8,128)(2,1)}), bf16[32,20,4096]{2,1,0:T(8,128)(2,1)}, u32[]{:S(2)}, u32[]{:S(2)}) %all-to-all-start.2) | async-done | bytes 5242912 | tf_op jit(solution)/shard_map/all_to_all | solution.py:117
  202.4 4.9 broadcast_in_dim.22
  207.3 20.9 %all-to-all-start.3 = ((bf16[32,20,4096]{2,1,0:T(8,128)(2,1)}), bf16[32,20,4096]{2,1,0:T(8,128)(2,1)}, u32[]{:S(2)}, u32[]{:S(2)}) async-start(bf16[32,20,4096]{2,1,0:T(8,128)(2,1)} %bitcast.69), calls=%async_computation.3 | async-start | bytes 12582912 | tf_op jit(solution)/shard_map/all_to_all | solution.py:116
  228.2 7.8 %reshape.209 = bf16[640,4096]{1,0:T(8,128)(2,1)} reshape(bf16[32,20,4096]{2,1,0:T(8,128)(2,1)} %all-to-all-done) | data formatting | bytes 10485760 | tf_op jit(solution)/shard_map/reshape | solution.py:47
  235.9 4.7 fusion.12
  240.6 0.0 copy-done
  240.6 11.0 %convolution_convert_fusion = bf16[640,4096]{1,0:T(8,128)(2,1)} fusion(bf16[1,256,4096]{2,1,0:T(8,128)(2,1)} %param.19, bf16[640,4096]{1,0:T(8,128)(2,1)} %reshape.209, bf16[1,4096,256]{2,1,0:T(8,128)(2,1)S(1)} %copy-done, f32[640,256]{1,0:T(8,128)S(1)} %fusion.12), kind=kOutput, calls=%fused_computation.3 | convolution fusion | flops 2687959040 | bytes 15335424 | tf_op jit(solution)/shard_map/dot_general | solution.py:51
  251.6 7.6 %reshape.210 = bf16[32,20,4096]{2,1,0:T(8,128)(2,1)} reshape(bf16[640,4096]{1,0:T(8,128)(2,1)} %convolution_convert_fusion) | data formatting | bytes 10485760 | tf_op jit(solution)/shard_map/reshape | solution.py:52
  259.2 47.6 %all-to-all-done.3 = bf16[32,20,4096]{2,1,0:T(8,128)(2,1)} async-done(((bf16[32,20,4096]{2,1,0:T(8,128)(2,1)}), bf16[32,20,4096]{2,1,0:T(8,128)(2,1)}, u32[]{:S(2)}, u32[]{:S(2)}) %all-to-all-start.3) | async-done | bytes 5242912 | tf_op jit(solution)/shard_map/all_to_all | solution.py:116
  306.8 17.9 %all-to-all-start.1 = ((bf16[32,20,4096]{2,1,0:T(8,128)(2,1)}), bf16[32,20,4096]{2,1,0:T(8,128)(2,1)}, u32[]{:S(2)}, u32[]{:S(2)}) async-start(bf16[32,20,4096]{2,1,0:T(8,128)(2,1)} %reshape.210), calls=%async_computation.1 | async-start | bytes 12582912 | tf_op jit(solution)/shard_map/all_to_all | solution.py:113
  324.7 7.7 %reshape.213 = bf16[640,4096]{1,0:T(8,128)(2,1)} reshape(bf16[32,20,4096]{2,1,0:T(8,128)(2,1)} %all-to-all-done.2) | data formatting | bytes 10485760 | tf_op jit(solution)/shard_map/reshape | solution.py:59
  332.5 7.8 %reshape.215 = bf16[640,4096]{1,0:T(8,128)(2,1)} reshape(bf16[32,20,4096]{2,1,0:T(8,128)(2,1)} %all-to-all-done.3) | data formatting | bytes 10485760 | tf_op jit(solution)/shard_map/reshape | solution.py:58
  340.3 4.8 fusion
  345.2 0.4 copy-done.5
  345.6 1.5 fusion.10
  347.2 12.6 %fusion.8 = f32[640,4096]{1,0:T(8,128)} fusion(bf16[1,4096,256]{2,1,0:T(8,128)(2,1)} %param.17, f32[640,256]{1,0:T(8,128)S(1)} %fusion, bf16[640,4096]{1,0:T(8,128)(2,1)} %reshape.215, bf16[1,4096,256]{2,1,0:T(8,128)(2,1)S(1)} %copy-done, f32[640,256]{1,0:T(8,128)S(1)} %fusion.10), kind=kOutput, calls=%fused_computation.15 | convolution fusion | flops 2685992960 | bytes 21233664 | tf_op jit(solution)/shard_map/dot_general | solution.py:40
  359.8 7.8 %add_convert_fusion = bf16[640,4096]{1,0:T(8,128)(2,1)} fusion(f32[640,4096]{1,0:T(8,128)} %fusion.8, bf16[1,4096,256]{2,1,0:T(8,128)(2,1)S(1)} %copy-done, f32[640,256]{1,0:T(8,128)S(1)} %fusion, f32[640,256]{1,0:T(8,128)S(1)} %fusion.10), kind=kOutput, calls=%fused_computation.2 | convolution fusion | flops 1348403200 | bytes 19136512 | tf_op jit(solution)/shard_map/dot_general | solution.py:40
  367.6 7.6 %reshape.216 = bf16[32,20,4096]{2,1,0:T(8,128)(2,1)} reshape(bf16[640,4096]{1,0:T(8,128)(2,1)} %add_convert_fusion) | data formatting | bytes 10485760 | tf_op jit(solution)/shard_map/reshape | solution.py:69
  375.3 27.9 %all-to-all-done.1 = bf16[32,20,4096]{2,1,0:T(8,128)(2,1)} async-done(((bf16[32,20,4096]{2,1,0:T(8,128)(2,1)}), bf16[32,20,4096]{2,1,0:T(8,128)(2,1)}, u32[]{:S(2)}, u32[]{:S(2)}) %all-to-all-start.1) | async-done | bytes 5242912 | tf_op jit(solution)/shard_map/all_to_all | solution.py:113
  403.2 11.5 %all-to-all-start.4 = ((bf16[32,20,4096]{2,1,0:T(8,128)(2,1)}), bf16[32,20,4096]{2,1,0:T(8,128)(2,1)}, u32[]{:S(2)}, u32[]{:S(2)}) async-start(bf16[32,20,4096]{2,1,0:T(8,128)(2,1)} %reshape.216), calls=%async_computation.4 | async-start | bytes 12582912 | tf_op jit(solution)/shard_map/all_to_all | solution.py:123
  414.7 0.1 compare_select_fusion.1
  414.8 0.1 reshape.220
  414.9 0.1 compare_select_fusion
  415.0 0.1 reshape.228
  415.1 7.8 %reshape.211 = bf16[640,4096]{1,0:T(8,128)(2,1)} reshape(bf16[32,20,4096]{2,1,0:T(8,128)(2,1)} %all-to-all-done.1) | data formatting | bytes 10485760 | tf_op jit(solution)/shard_map/reshape | solution.py:74
  422.9 11.7 %gather_fusion = bf16[512,4096]{1,0:T(8,128)(2,1)} fusion(bf16[640,4096]{1,0:T(8,128)(2,1)} %reshape.211, s32[1024]{0:T(1024)S(1)} %pad_clamp_fusion.1), kind=kCustom, calls=%fused_computation | custom fusion | bytes 8390656 | tf_op jit(solution)/shard_map/gather | solution.py:77
  434.6 8.3 %reshape.236 = f32[128,4,4096]{2,1,0:T(4,128)} reshape(bf16[512,4096]{1,0:T(8,128)(2,1)} %gather_fusion) | data formatting | bytes 12582912 | tf_op jit(solution)/shard_map/convert_element_type | solution.py:77
  442.9 8.8 %reduce_sum.37 = f32[128,4096]{1,0:T(8,128)S(1)} reduce(f32[128,4,4096]{2,1,0:T(4,128)} %reshape.236, f32[]{:T(128)} %constant.21.clone.1), dimensions={1}, to_apply=%region_2.3 | reduce | flops 1572864 | bytes 10485764 | tf_op jit(solution)/shard_map/reduce_sum | solution.py:77
  451.7 0.0 copy-done.3
  451.7 0.0 copy-done.7
  451.7 1.3 add_convert_fusion.2
  453.0 5.8 collective-permute-start
  458.8 44.8 %all-to-all-done.4 = bf16[32,20,4096]{2,1,0:T(8,128)(2,1)} async-done(((bf16[32,20,4096]{2,1,0:T(8,128)(2,1)}), bf16[32,20,4096]{2,1,0:T(8,128)(2,1)}, u32[]{:S(2)}, u32[]{:S(2)}) %all-to-all-start.4) | async-done | bytes 5242912 | tf_op jit(solution)/shard_map/all_to_all | solution.py:123
  503.5 7.7 %reshape.217 = bf16[640,4096]{1,0:T(8,128)(2,1)} reshape(bf16[32,20,4096]{2,1,0:T(8,128)(2,1)} %all-to-all-done.4) | data formatting | bytes 10485760 | tf_op jit(solution)/shard_map/reshape | solution.py:74
  511.2 11.8 %gather_fusion.1 = bf16[512,4096]{1,0:T(8,128)(2,1)} fusion(bf16[640,4096]{1,0:T(8,128)(2,1)} %reshape.217, s32[1024]{0:T(1024)S(1)} %pad_clamp_fusion), kind=kCustom, calls=%fused_computation.1 | custom fusion | bytes 8390656 | tf_op jit(solution)/shard_map/gather | solution.py:77
  523.0 8.4 %reshape.237 = f32[128,4,4096]{2,1,0:T(4,128)} reshape(bf16[512,4096]{1,0:T(8,128)(2,1)} %gather_fusion.1) | data formatting | bytes 12582912 | tf_op jit(solution)/shard_map/convert_element_type | solution.py:77
  531.5 10.1 %reduce_sum.39 = f32[128,4096]{1,0:T(8,128)} reduce(f32[128,4,4096]{2,1,0:T(4,128)} %reshape.237, f32[]{:T(128)} %constant.21.clone.1), dimensions={1}, to_apply=%region_5.6 | reduce | flops 1572864 | bytes 10485764 | tf_op jit(solution)/shard_map/reduce_sum | solution.py:77
  541.5 0.0 copy-done.4
  541.5 2.1 add_convert_fusion.1
  543.6 6.3 %collective-permute-start.1 = (bf16[128,4096]{1,0:T(8,128)(2,1)S(1)}, bf16[128,4096]{1,0:T(8,128)(2,1)S(1)}, u32[]{:S(2)}, u32[]{:S(2)}) collective-permute-start(bf16[128,4096]{1,0:T(8,128)(2,1)S(1)} %add_convert_fusion.1), channel_id=1, source_target_pairs={{0,224},{32,0},{64,32},{96,64},{128,96},{160,128},{192,160},{224,1... | collective-permute-start | bytes 3145736 | tf_op jit(solution)/shard_map/ppermute | solution.py:13
  549.9 0.0 collective-permute-done
  549.9 26.9 %collective-permute-done.1 = bf16[128,4096]{1,0:T(8,128)(2,1)S(1)} collective-permute-done((bf16[128,4096]{1,0:T(8,128)(2,1)S(1)}, bf16[128,4096]{1,0:T(8,128)(2,1)S(1)}, u32[]{:S(2)}, u32[]{:S(2)}) %collective-permute-start.1) | collective-permute-done | bytes 1048608 | tf_op jit(solution)/shard_map/ppermute | solution.py:13
  576.8 2.3 copy.14
  579.1 1.0 copy.15
  (14 shorter events, 0.0 us)
Async XLA Ops:
  0.6 240.0 %copy-start = (bf16[1,4096,256]{2,1,0:T(8,128)(2,1)S(1)}, bf16[1,4096,256]{2,1,0:T(8,128)(2,1)}, u32[]{:S(2)}) copy-start(bf16[1,4096,256]{2,1,0:T(8,128)(2,1)} %param.18) | copy-start | bytes 6291460
  11.1 8.1 %copy-start.6 = (s32[1,128,1]{1,2,0:T(1,128)S(1)}, s32[1,128,1]{1,2,0:T(1,128)}, u32[]{:S(2)}) copy-start(s32[1,128,1]{1,2,0:T(1,128)} %param.14) | copy-start | bytes 1540
  11.1 93.4 %all-to-all-start = ((bf16[32,20,4096]{2,1,0:T(8,128)(2,1)}), bf16[32,20,4096]{2,1,0:T(8,128)(2,1)}, u32[]{:S(2)}, u32[]{:S(2)}) async-start(bf16[32,20,4096]{2,1,0:T(8,128)(2,1)} %bitcast.68), calls=%async_computation | async-start | bytes 12582912 | tf_op jit(solution)/shard_map/all_to_all | solution.py:108
  109.3 93.1 %all-to-all-start.2 = ((bf16[32,20,4096]{2,1,0:T(8,128)(2,1)}), bf16[32,20,4096]{2,1,0:T(8,128)(2,1)}, u32[]{:S(2)}, u32[]{:S(2)}) async-start(bf16[32,20,4096]{2,1,0:T(8,128)(2,1)} %bitcast.70), calls=%async_computation.2 | async-start | bytes 12582912 | tf_op jit(solution)/shard_map/all_to_all | solution.py:117
  207.3 99.5 %all-to-all-start.3 = ((bf16[32,20,4096]{2,1,0:T(8,128)(2,1)}), bf16[32,20,4096]{2,1,0:T(8,128)(2,1)}, u32[]{:S(2)}, u32[]{:S(2)}) async-start(bf16[32,20,4096]{2,1,0:T(8,128)(2,1)} %bitcast.69), calls=%async_computation.3 | async-start | bytes 12582912 | tf_op jit(solution)/shard_map/all_to_all | solution.py:116
  306.8 96.4 %all-to-all-start.1 = ((bf16[32,20,4096]{2,1,0:T(8,128)(2,1)}), bf16[32,20,4096]{2,1,0:T(8,128)(2,1)}, u32[]{:S(2)}, u32[]{:S(2)}) async-start(bf16[32,20,4096]{2,1,0:T(8,128)(2,1)} %reshape.210), calls=%async_computation.1 | async-start | bytes 12582912 | tf_op jit(solution)/shard_map/all_to_all | solution.py:113
  340.3 4.9 copy-start.2
  340.3 5.3 copy-start.5
  403.2 100.3 %all-to-all-start.4 = ((bf16[32,20,4096]{2,1,0:T(8,128)(2,1)}), bf16[32,20,4096]{2,1,0:T(8,128)(2,1)}, u32[]{:S(2)}, u32[]{:S(2)}) async-start(bf16[32,20,4096]{2,1,0:T(8,128)(2,1)} %reshape.216), calls=%async_computation.4 | async-start | bytes 12582912 | tf_op jit(solution)/shard_map/all_to_all | solution.py:123
  442.9 8.8 %copy-start.3 = (bf16[1,128,4096]{2,1,0:T(8,128)(2,1)S(1)}, bf16[1,128,4096]{2,1,0:T(8,128)(2,1)}, u32[]{:S(2)}) copy-start(bf16[1,128,4096]{2,1,0:T(8,128)(2,1)} %param.10) | copy-start | bytes 3145732
  442.9 8.8 %copy-start.7 = (f32[1,128,1]{1,2,0:T(1,128)S(1)}, f32[1,128,1]{1,2,0:T(1,128)}, u32[]{:S(2)}) copy-start(f32[1,128,1]{1,2,0:T(1,128)} %param.12) | copy-start | bytes 1540
  453.0 96.9 %collective-permute-start = (bf16[128,4096]{1,0:T(8,128)(2,1)}, bf16[128,4096]{1,0:T(8,128)(2,1)}, u32[]{:S(2)}, u32[]{:S(2)}) collective-permute-start(bf16[128,4096]{1,0:T(8,128)(2,1)} %add_convert_fusion.2), channel_id=1, source_target_pairs={{0,32},{32,64},{64,96},{96,128},{128,160},{160,192},{192,224},{224... | collective-permute-start | bytes 3145736 | tf_op jit(solution)/shard_map/ppermute | solution.py:13
  531.5 10.1 %copy-start.4 = (bf16[1,128,4096]{2,1,0:T(8,128)(2,1)S(1)}, bf16[1,128,4096]{2,1,0:T(8,128)(2,1)}, u32[]{:S(2)}) copy-start(bf16[1,128,4096]{2,1,0:T(8,128)(2,1)} %param.16) | copy-start | bytes 3145732
  531.5 10.1 %copy-start.8 = (f32[1,128,1]{1,2,0:T(1,128)S(1)}, f32[1,128,1]{1,2,0:T(1,128)}, u32[]{:S(2)}) copy-start(f32[1,128,1]{1,2,0:T(1,128)} %param.15) | copy-start | bytes 1540
  541.5 38.5 %copy-start.1 = (bf16[1,4096,256]{2,1,0:T(8,128)(2,1)S(1)}, bf16[1,4096,256]{2,1,0:T(8,128)(2,1)}, u32[]{:S(2)}) copy-start(bf16[1,4096,256]{2,1,0:T(8,128)(2,1)} %param.18) | copy-start | bytes 6291460
  543.6 33.2 %collective-permute-start.1 = (bf16[128,4096]{1,0:T(8,128)(2,1)S(1)}, bf16[128,4096]{1,0:T(8,128)(2,1)S(1)}, u32[]{:S(2)}, u32[]{:S(2)}) collective-permute-start(bf16[128,4096]{1,0:T(8,128)(2,1)S(1)} %add_convert_fusion.1), channel_id=1, source_target_pairs={{0,224},{32,0},{64,32},{96,64},{128,96},{160,128},{192,160},{224,1... | collective-permute-start | bytes 3145736 | tf_op jit(solution)/shard_map/ppermute | solution.py:13
where the time goes:
time: 591 us; the launch traced here: 580 us
  waiting for transfers between devices  305 us (52%)
  local copies, waits for them, and re-layouts  117 us (20%)
  starting transfers between devices  84.8 us (14%)
  matrix products  47.7 us (8%)
  other arithmetic  25.4 us (4%)
    all_to_all x1, waiting for transfers between devices, on_device(): lax.all_to_all(send_fwd, 'expert', split_axis=0, concat_axis=0, tiled=True)  81.8 us
    all_to_all x1, waiting for transfers between devices, on_device(): lax.all_to_all(send_grads, 'expert', split_axis=0, concat_axis=0, tiled=T...  75.7 us
    all_to_all x2, waiting for transfers between devices, on_device(): lax.all_to_all(partial_value, 'expert', split_axis=0, concat_axis=0, tile...  72.7 us
    all_to_all x1, waiting for transfers between devices, on_device(): lax.all_to_all(send_inputs, 'expert', split_axis=0, concat_axis=0, tiled=...  47.6 us
    all_to_all x2, starting transfers between devices, on_device(): lax.all_to_all(partial_value, 'expert', split_axis=0, concat_axis=0, tile...  29.4 us
    ppermute x2, waiting for transfers between devices, shifted(): return lax.ppermute(value, axis, pairs)  26.9 us
    dot_general x3, matrix products, contract_last(): lax.dot_general(left, right, (((1,), (1,)), ((), ())), preferred_element_...  25.3 us
    gather x2, local copies, waits for them, and re-layouts, collect_direct(): return jnp.sum(flat_rows[where_rows].astype(jnp.float32), axis=1)  23.6 us
  transfers between devices with their start and end apart: 7, of which 6 were waited for; matrix products, arithmetic and copies ran while one was open for 29% of the time, Pallas kernels for 0%

commit v1 on v0

v1 whole, which is shorter than its diff:
```python
import functools

import jax
import jax.numpy as jnp
from jax import lax
from jax.experimental import pallas as pl
from jax.experimental.pallas import tpu as pltpu
from jax.sharding import PartitionSpec as P

MESH = pl.DeviceIdType.MESH
F32 = jnp.float32
BF16 = jnp.bfloat16

GROUP = 4
SLOTS = 16
EXTRA = 4
CHUNKS = 4


def dot(left, right):
    return jnp.dot(left, right, preferred_element_type=F32)


def dot_last(left, right):
    return lax.dot_general(left, right, (((1,), (1,)), ((), ())), preferred_element_type=F32)


def iota(shape, dim):
    return lax.broadcasted_iota(jnp.int32, shape, dim)


def multiple(value, of):
    return pl.multiple_of(value, of)


def kernel(
    experts,
    pipes,
    fwd_in,
    bwd_in,
    cot_in,
    w_gate,
    w_up,
    w_down,
    fwd_route,
    bwd_route,
    fwd_prob,
    bwd_prob,
    next_fwd,
    next_cot,
    rows_in,
    packed,
    tokens,
    gate,
    up,
    down,
    stack,
    acc,
    hidden,
    grads,
    mine,
    theirs,
    others,
    summed,
    back,
    final,
    sel_in,
    sel_out,
    unfold,
    fold,
    local_sem,
    w_send,
    w_recv,
    d_send,
    d_recv,
    t_send,
    t_recv,
    c_send,
    c_recv,
    r_send,
    r_recv,
    p_send,
    p_recv,
):
    tok, width = rows_in.shape[1], rows_in.shape[2]
    part = width // CHUNKS
    quarter = part // EXTRA
    hdev = gate.shape[2]
    main = experts * SLOTS

    section = lax.axis_index("pipe")
    member = lax.axis_index("expert")
    core = section % 2
    x = member % GROUP
    me = member // GROUP
    pair_a = x + 1 - 2 * (x % 2)
    pair_b = GROUP - 1 - x
    token_mate = (section, me * GROUP + (1 - core) * pair_a + core * pair_b)
    weight_mate = (section, me * GROUP + core * pair_a + (1 - core) * pair_b)
    upstream = ((section + 1) % pipes, member)
    downstream = ((section + pipes - 1) % pipes, member)

    def peer(k):
        return (me + k) % experts

    def remote(src, dst, send, recv, device):
        return pltpu.make_async_remote_copy(
            src_ref=src, dst_ref=dst, send_sem=send, recv_sem=recv, device_id=device, device_id_type=MESH
        )

    def cols(c):
        return pl.ds(multiple(c * part, part), part)

    def weight_copy(i, c):
        if i < 2:
            src, dst = ((w_gate, gate), (w_up, up))[i]
            return remote(
                src.at[0, cols(c)], dst.at[1, cols(c)], w_send.at[i, c], w_recv.at[i, c], weight_mate
            )
        return remote(
            w_down.at[0, :, cols(c)],
            down.at[c, pl.ds(hdev, hdev)],
            w_send.at[i, c],
            w_recv.at[i, c],
            weight_mate,
        )

    def slot_rows(k):
        return pl.ds(multiple(k * SLOTS, SLOTS), SLOTS)

    def spread_copy(src, dst, send, recv, i, c, k):
        to = peer(k)
        return remote(
            src.at[i, c, slot_rows(to)],
            dst.at[i, c, slot_rows(me)],
            send.at[i, c, k],
            recv.at[i, c, k],
            (section, to * GROUP + x),
        )

    def dispatch(i, c, k):
        return spread_copy(packed, tokens, d_send, d_recv, i, c, k)

    def give_back(i, c, k):
        return spread_copy(summed, back, r_send, r_recv, i, c, k)

    def mate_copy(i, c):
        return remote(
            tokens.at[i, c, pl.ds(0, main)],
            tokens.at[i, c, pl.ds(main, main)],
            t_send.at[i, c],
            t_recv.at[i, c],
            token_mate,
        )

    def result_copy(i, c):
        return remote(theirs.at[i, c], others.at[i, c], c_send.at[i, c], c_recv.at[i, c], token_mate)

    def relay_copy(i, c):
        out = (next_fwd, next_cot)[i]
        return remote(
            final.at[i, c],
            out.at[0, :, cols(c)],
            p_send.at[i, c],
            p_recv.at[i, c],
            (upstream, downstream)[i],
        )

    def each(body, count=CHUNKS):
        lax.fori_loop(0, count, lambda c, carry: (body(c), carry)[1], 0)

    local = [
        pltpu.make_async_copy(src.at[0], rows_in.at[i], local_sem.at[i])
        for i, src in enumerate((fwd_in, bwd_in, cot_in))
    ]
    local.append(pltpu.make_async_copy(w_gate.at[0], gate.at[0], local_sem.at[3]))
    local.append(pltpu.make_async_copy(w_up.at[0], up.at[0], local_sem.at[4]))
    for c in range(CHUNKS):
        local.append(
            pltpu.make_async_copy(
                w_down.at[0, :, pl.ds(c * part, part)], down.at[c, pl.ds(0, hdev)], local_sem.at[5 + c]
            )
        )
    for copy in local:
        copy.start()

    barrier = pltpu.get_barrier_semaphore()
    greeted = [(section, peer(k) * GROUP + x) for k in range(1, experts)]
    greeted += [token_mate, weight_mate, upstream, downstream]
    for device in greeted:
        pl.semaphore_signal(barrier, inc=1, device_id=device, device_id_type=MESH)

    def select(o, route):
        ids = route[0]
        lane = iota((tok, main), 1)
        token = iota((tok, main), 0)
        onehot = (lane == ids).astype(F32).astype(BF16)
        earlier = (lane < token).astype(F32).astype(BF16)
        before = dot(earlier, onehot)
        place = jnp.sum(before * onehot.astype(F32), axis=1, keepdims=True)
        lane_f = lane.astype(F32)
        first = ids.astype(F32) * SLOTS
        whole = jnp.where(place < SLOTS, first + place, -1.0)
        chosen = (whole == lane_f).astype(F32)
        sel_in[o, 0] = chosen.T.astype(BF16)
        for q in range(EXTRA):
            sel_out[o, q, :, 0:main] = chosen.astype(BF16)
        for q in range(EXTRA):
            folded = jnp.where(place >= SLOTS, first + (place - SLOTS) + q * EXTRA, -1.0)
            chosen = (folded == lane_f).astype(F32)
            sel_in[o, 1 + q] = chosen.T.astype(BF16)
            sel_out[o, q, :, main : 2 * main] = chosen.astype(BF16)

    select(0, fwd_route)
    select(1, bwd_route)

    extra = experts * EXTRA
    for q in range(EXTRA):
        r = iota((2 * extra, 2 * main), 0)
        i = iota((2 * extra, 2 * main), 1)
        unfold[q] = (i == (r // EXTRA) * SLOTS + q * EXTRA + r % EXTRA).astype(F32).astype(BF16)
        r = iota((2 * main, 2 * extra), 1)
        i = iota((2 * main, 2 * extra), 0)
        fold[q] = (i == (r // EXTRA) * SLOTS + q * EXTRA + r % EXTRA).astype(F32).astype(BF16)
    acc[...] = jnp.zeros_like(acc)

    pl.semaphore_wait(barrier, len(greeted))
    for i in range(3):
        each(lambda c: weight_copy(i, c).start())

    for i in range(3):
        o = min(i, 1)
        local[i].wait()

        def pack(c, i=i, o=o):
            rows = rows_in[i, :, cols(c)]
            packed[i, c, :, 0:part] = dot(sel_in[o, 0], rows).astype(BF16)
            total = dot(sel_in[o, 1], rows[:, 0:quarter])
            for q in range(1, EXTRA):
                total += dot(sel_in[o, 1 + q], rows[:, q * quarter : (q + 1) * quarter])
            packed[i, c, :, part:] = total.astype(BF16)
            for k in range(1, experts):
                dispatch(i, c, k).start()
            tokens[i, c, slot_rows(me)] = packed[i, c, slot_rows(me)]

        each(pack)

    for i in range(3):

        def pass_on(c, i=i):
            for k in range(1, experts):
                dispatch(i, c, k).wait_recv()
            mate_copy(i, c).start()

        each(pass_on)

    for copy in local[3:]:
        copy.wait()

    def load(i, c):
        stack[0 : 2 * main] = tokens[i, c, :, 0:part]
        folded = tokens[i, c, :, part:]
        for q in range(EXTRA):
            stack[2 * main :, q * quarter : (q + 1) * quarter] = dot(unfold[q], folded).astype(BF16)

    def store(o, c, value):
        mine[o, c, :, 0:part] = value[0:main].astype(BF16)
        theirs[o, c, :, 0:part] = value[main : 2 * main].astype(BF16)
        rest = value[2 * main :].astype(BF16)
        total = dot(fold[0], rest[:, 0:quarter])
        for q in range(1, EXTRA):
            total += dot(fold[q], rest[:, q * quarter : (q + 1) * quarter])
        mine[o, c, :, part:] = total[0:main].astype(BF16)
        theirs[o, c, :, part:] = total[main:].astype(BF16)
        result_copy(o, c).start()

    def project(i, c):
        load(i, c)
        for half in range(2):
            at = pl.ds(half * hdev, hdev)
            acc[2 * i, :, at] += dot(stack[...], gate[half, cols(c)])
            acc[2 * i + 1, :, at] += dot(stack[...], up[half, cols(c)])

    def forward_in_step(c):
        mate_copy(0, c).wait_recv()
        weight_copy(0, c).wait_recv()
        weight_copy(1, c).wait_recv()
        project(0, c)

    each(forward_in_step)
    gate_pre = acc[0]
    hidden[...] = (gate_pre / (1.0 + jnp.exp(-gate_pre)) * acc[1]).astype(BF16)

    def backward_in_step(c):
        mate_copy(1, c).wait_recv()
        project(1, c)

    each(backward_in_step)

    def down_step(c):
        weight_copy(2, c).wait_recv()
        store(0, c, dot(hidden[...], down[c]))
        mate_copy(2, c).wait_recv()
        load(2, c)
        acc[4] += dot_last(stack[...], down[c])

    each(down_step)

    back_gate = acc[2]
    back_hid = acc[4]
    g = 1.0 / (1.0 + jnp.exp(-back_gate))
    grads[0] = (back_hid * acc[3] * g * (1.0 + back_gate * (1.0 - g))).astype(BF16)
    grads[1] = (back_hid * back_gate * g).astype(BF16)

    def return_step(o, c):
        result_copy(o, c).wait_recv()
        summed[o, c] = (mine[o, c].astype(F32) + others[o, c].astype(F32)).astype(BF16)
        for k in range(1, experts):
            give_back(o, c, k).start()
        back[o, c, slot_rows(me)] = summed[o, c, slot_rows(me)]

    def backward_step(c):
        total = dot_last(grads[0, :, 0:hdev], gate[0, cols(c)])
        total += dot_last(grads[0, :, hdev:], gate[1, cols(c)])
        total += dot_last(grads[1, :, 0:hdev], up[0, cols(c)])
        total += dot_last(grads[1, :, hdev:], up[1, cols(c)])
        store(1, c, total)
        return_step(0, c)

    each(backward_step)

    def finish(o, c):
        for k in range(1, experts):
            give_back(o, c, k).wait_recv()
        prob = (fwd_prob, bwd_prob)[o][0]
        res = 2 * o
        for q in range(EXTRA):
            at = pl.ds(multiple(c * part + q * quarter, quarter), quarter)
            branch = dot(sel_out[o, q, :, 0:main], back[o, c, :, q * quarter : (q + 1) * quarter])
            branch += dot(sel_out[o, q, :, main:], back[o, c, :, part:])
            value = rows_in[res, :, at].astype(F32) + prob * branch
            final[o, c, :, q * quarter : (q + 1) * quarter] = value.astype(BF16)
        relay_copy(o, c).start()

    def end_step(c):
        finish(0, c)
        return_step(1, c)

    each(end_step)
    each(lambda c: finish(1, c))

    def drain(c):
        for i in range(3):
            weight_copy(i, c).wait_send()
            mate_copy(i, c).wait_send()
            for k in range(1, experts):
                dispatch(i, c, k).wait_send()
        for o in range(2):
            result_copy(o, c).wait_send()
            for k in range(1, experts):
                give_back(o, c, k).wait_send()
            relay_copy(o, c).wait()

    each(drain)


def on_device(
    forward_in,
    forward_route,
    forward_gate_prob,
    backward_in,
    backward_route,
    backward_gate_prob,
    cotangent,
    w_gate,
    w_up,
    w_down,
):
    experts = lax.axis_size("expert") // GROUP
    pipes = lax.axis_size("pipe")
    _, tok, width = forward_in.shape
    hdev = w_gate.shape[2]
    main = experts * SLOTS
    extra = experts * EXTRA
    part = width // CHUNKS
    wide = part + part // EXTRA
    rows = 2 * (main + extra)
    hbm = pl.BlockSpec(memory_space=pl.ANY)
    vmem = pl.BlockSpec(memory_space=pltpu.VMEM)
    dma = pltpu.SemaphoreType.DMA
    return pl.pallas_call(
        functools.partial(kernel, experts, pipes),
        out_shape=[jax.ShapeDtypeStruct(forward_in.shape, BF16)] * 2,
        in_specs=[hbm] * 6 + [vmem] * 4,
        out_specs=[hbm] * 2,
        scratch_shapes=[
            pltpu.VMEM((3, tok, width), BF16),
            pltpu.VMEM((3, CHUNKS, main, wide), BF16),
            pltpu.VMEM((3, CHUNKS, 2 * main, wide), BF16),
            pltpu.VMEM((2, width, hdev), BF16),
            pltpu.VMEM((2, width, hdev), BF16),
            pltpu.VMEM((CHUNKS, 2 * hdev, part), BF16),
            pltpu.VMEM((rows, part), BF16),
            pltpu.VMEM((5, rows, 2 * hdev), F32),
            pltpu.VMEM((rows, 2 * hdev), BF16),
            pltpu.VMEM((2, rows, 2 * hdev), BF16),
            pltpu.VMEM((2, CHUNKS, main, wide), BF16),
            pltpu.VMEM((2, CHUNKS, main, wide), BF16),
            pltpu.VMEM((2, CHUNKS, main, wide), BF16),
            pltpu.VMEM((2, CHUNKS, main, wide), BF16),
            pltpu.VMEM((2, CHUNKS, main, wide), BF16),
            pltpu.VMEM((2, CHUNKS, tok, part), BF16),
            pltpu.VMEM((2, 1 + EXTRA, main, tok), BF16),
            pltpu.VMEM((2, EXTRA, tok, 2 * main), BF16),
            pltpu.VMEM((EXTRA, 2 * extra, 2 * main), BF16),
            pltpu.VMEM((EXTRA, 2 * main, 2 * extra), BF16),
            dma((5 + CHUNKS,)),
            dma((3, CHUNKS)),
            dma((3, CHUNKS)),
            dma((3, CHUNKS, experts)),
            dma((3, CHUNKS, experts)),
            dma((3, CHUNKS)),
            dma((3, CHUNKS)),
            dma((2, CHUNKS)),
            dma((2, CHUNKS)),
            dma((2, CHUNKS, experts)),
            dma((2, CHUNKS, experts)),
            dma((2, CHUNKS)),
            dma((2, CHUNKS)),
        ],
        compiler_params=pltpu.CompilerParams(
            collective_id=1, has_side_effects=True, vmem_limit_bytes=60 * 2**20
        ),
    )(
        forward_in,
        backward_in,
        cotangent,
        w_gate,
        w_up,
        w_down,
        forward_route,
        backward_route,
        forward_gate_prob,
        backward_gate_prob,
    )


def solution(mesh):
    tokens = P("pipe", "expert", None)
    columns = P("pipe", None, "expert")
    return jax.shard_map(
        lambda *args: tuple(on_device(*args)),
        mesh=mesh,
        in_specs=(tokens,) * 7 + (columns, columns, tokens),
        out_specs=(tokens, tokens),
        check_vma=False,
    )
```

time: 591 us -> 209 us (0.35)
  the two profiles are of different devices: /device:TPU:43 before, /device:TPU:1 now
where the time goes in v1:
time: 209 us; the launch traced here: 206 us
  Pallas kernels  197 us (94%)
  local copies, waits for them, and re-layouts  8.89 us (4%)
    pallas_call x1, Pallas kernels, on_device(): pl.pallas_call(functools.partial(kernel, experts, pipes), out_shape=[jax....  197 us
    unnamed x8, local copies, waits for them, and re-layouts  8.89 us

profile of v1, /device:TPU:1, one launch (start us, length us, event | category | flops | bytes accessed | tf_op | source)
XLA Modules:
  0.0 206.4 jit_solution(1226720864306485743)
XLA Ops:
  0.6 1.4 copy.12.fwd_route
  2.0 1.4 copy.14.fwd_prob
  3.4 1.4 copy.13.bwd_route
  4.8 1.4 copy.15.bwd_prob
  6.2 196.8 %shard_map.113 = (bf16[1,128,4096]{2,1,0:T(8,128)(2,1)}, bf16[1,128,4096]{2,1,0:T(8,128)(2,1)}) custom-call(bf16[1,128,4096]{2,1,0:T(8,128)(2,1)} %fwd_in.1, bf16[1,128,4096]{2,1,0:T(8,128)(2,1)} %bwd_in.1, bf16[1,128,4096]{2,1,0:T(8,128)(2,1)} %cot_in.1, bf16[1,4096,256]{2,1,0:T(8,128)(2,1)} %w_gate.1, bf16[1,4096,256]{2,1,0:T(8,128)(2,1)} %w_up.1, ...), custom_call_target="tpu_custom_call" | custom-call | tf_op jit(solution)/shard_map/pallas_call | solution.py:391
  203.0 0.0 copy-start
  203.0 2.4 %copy.18 = bf16[1,128,4096]{2,1,0:T(8,128)(2,1)} copy(bf16[1,128,4096]{2,1,0:T(8,128)(2,1)} %get-tuple-element.4) | data formatting | bytes 2097152
  205.4 0.0 copy-done
  205.4 1.0 copy.19
Async XLA Ops:
  203.0 2.4 %copy-start = (bf16[1,128,4096]{2,1,0:T(8,128)(2,1)S(1)}, bf16[1,128,4096]{2,1,0:T(8,128)(2,1)}, u32[]{:S(2)}) copy-start(bf16[1,128,4096]{2,1,0:T(8,128)(2,1)} %get-tuple-element.5) | copy-start | bytes 3145732

commit v2 on v1

v2 whole, which is shorter than its diff:
```python
import functools

import jax
import jax.numpy as jnp
from jax import lax
from jax.experimental import pallas as pl
from jax.experimental.pallas import tpu as pltpu
from jax.sharding import PartitionSpec as P

MESH = pl.DeviceIdType.MESH
F32 = jnp.float32
BF16 = jnp.bfloat16

GROUP = 4
SLOTS = 16
EXTRA = 4
CHUNKS = 4
SETS = 2


def dot(left, right):
    return jnp.dot(left, right, preferred_element_type=F32)


def dot_last(left, right):
    return lax.dot_general(left, right, (((1,), (1,)), ((), ())), preferred_element_type=F32)


def iota(shape, dim):
    return lax.broadcasted_iota(jnp.int32, shape, dim)


def multiple(value, of):
    return pl.multiple_of(value, of)


def kernel(
    experts,
    pipes,
    fwd_in,
    bwd_in,
    cot_in,
    w_gate,
    w_up,
    w_down,
    fwd_route,
    bwd_route,
    fwd_prob,
    bwd_prob,
    next_fwd,
    next_cot,
    rows_in,
    packed,
    tokens,
    gate,
    up,
    down,
    stack,
    acc,
    hidden,
    grads,
    mine,
    theirs,
    others,
    summed,
    back,
    resid,
    far_route,
    far_prob,
    prob,
    final,
    sel_in,
    sel_out,
    unfold,
    fold,
    local_sem,
    w_send,
    w_recv,
    d_send,
    d_recv,
    t_send,
    t_recv,
    c_send,
    c_recv,
    r_send,
    r_recv,
    m_send,
    m_recv,
    out_sem,
):
    tok, width = rows_in.shape[1], rows_in.shape[2]
    part = width // CHUNKS
    quarter = part // EXTRA
    hdev = gate.shape[2]
    main = experts * SLOTS
    members = experts // SETS
    block = members * SLOTS

    section = lax.axis_index("pipe")
    member = lax.axis_index("expert")
    core = section % 2
    x = member % GROUP
    me = member // GROUP
    pair_a = x + 1 - 2 * (x % 2)
    pair_b = GROUP - 1 - x
    token_mate = (section, me * GROUP + (1 - core) * pair_a + core * pair_b)
    weight_mate = (section, me * GROUP + core * pair_a + (1 - core) * pair_b)
    ahead = (section + 1) % pipes
    behind = (section + pipes - 1) % pipes

    def peer(k):
        return (me + k) % experts

    def set_of(j):
        return (j // 4 + j) % SETS

    def place_of(j):
        return j // SETS

    def source(s, place):
        z = (place * SETS) // 4
        return place * SETS + (s + z) % SETS

    def remote(src, dst, send, recv, device):
        return pltpu.make_async_remote_copy(
            src_ref=src, dst_ref=dst, send_sem=send, recv_sem=recv, device_id=device, device_id_type=MESH
        )

    def cols(c):
        return pl.ds(multiple(c * part, part), part)

    def slot_rows(k):
        return pl.ds(multiple(k * SLOTS, SLOTS), SLOTS)

    def weight_copy(i, c):
        if i < 2:
            held = (gate, up)[i]
            return remote(
                held.at[0, cols(c)], held.at[1, cols(c)], w_send.at[i, c], w_recv.at[i, c], weight_mate
            )
        return remote(
            down.at[c, pl.ds(0, hdev)],
            down.at[c, pl.ds(hdev, hdev)],
            w_send.at[i, c],
            w_recv.at[i, c],
            weight_mate,
        )

    def dispatch(i, c, k):
        to = peer(k)
        return remote(
            packed.at[i, c, slot_rows(to)],
            tokens.at[i, set_of(me), c, slot_rows(place_of(me))],
            d_send.at[i, c, k],
            d_recv.at[i, c, me],
            (section, to * GROUP + x),
        )

    def dispatch_from(i, c, j):
        return remote(
            packed.at[i, c, slot_rows(j)],
            tokens.at[i, set_of(j), c, slot_rows(place_of(j))],
            d_send.at[i, c, 0],
            d_recv.at[i, c, j],
            (section, j * GROUP + x),
        )

    def mate_copy(i, s, c):
        return remote(
            tokens.at[i, s, c, pl.ds(0, block)],
            tokens.at[i, s, c, pl.ds(block, block)],
            t_send.at[i, s, c],
            t_recv.at[i, s, c],
            token_mate,
        )

    def result_copy(o, s, c):
        return remote(
            theirs.at[o, s, c], others.at[o, s, c], c_send.at[o, s, c], c_recv.at[o, s, c], token_mate
        )

    def give(o, s, c, place):
        j = source(s, place)
        return remote(
            summed.at[o, s, c, slot_rows(place)],
            back.at[o, c, slot_rows(me)],
            r_send.at[o, c, j],
            r_recv.at[o, c, me],
            ((ahead, behind)[o], j * GROUP + x),
        )

    def give_from(o, c, j):
        return remote(
            summed.at[o, 0, c, slot_rows(0)],
            back.at[o, c, slot_rows(j)],
            r_send.at[o, c, j],
            r_recv.at[o, c, j],
            ((ahead, behind)[o], j * GROUP + x),
        )

    def message(i, o):
        src, dst = (
            ((fwd_in, cot_in)[o].at[0], resid.at[o]),
            ((fwd_route, bwd_route)[o], far_route.at[o]),
            ((fwd_prob, bwd_prob)[o], far_prob.at[o]),
        )[i]
        return remote(src, dst, m_send.at[i, o], m_recv.at[i, o], ((ahead, behind)[o], member))

    def out_copy(o, c):
        out = (next_fwd, next_cot)[o]
        return pltpu.make_async_copy(final.at[o, c], out.at[0, :, cols(c)], out_sem.at[o, c])

    def each(body, count=CHUNKS):
        lax.fori_loop(0, count, lambda c, carry: (body(c), carry)[1], 0)

    local = [
        pltpu.make_async_copy(src.at[0], rows_in.at[i], local_sem.at[i])
        for i, src in enumerate((fwd_in, bwd_in, cot_in))
    ]
    local.append(pltpu.make_async_copy(w_gate.at[0], gate.at[0], local_sem.at[3]))
    local.append(pltpu.make_async_copy(w_up.at[0], up.at[0], local_sem.at[4]))
    for c in range(CHUNKS):
        local.append(
            pltpu.make_async_copy(
                w_down.at[0, :, pl.ds(c * part, part)], down.at[c, pl.ds(0, hdev)], local_sem.at[5 + c]
            )
        )
    for copy in local[3:5] + local[:3] + local[5:]:
        copy.start()

    barrier = pltpu.get_barrier_semaphore()

    def greet(device):
        pl.semaphore_signal(barrier, inc=1, device_id=device, device_id_type=MESH)

    greet(token_mate)
    greet(weight_mate)
    each(lambda k: greet((section, peer(k + 1) * GROUP + x)), experts - 1)
    each(lambda k: greet((ahead, k * GROUP + x)), experts)
    each(lambda k: greet((behind, k * GROUP + x)), experts)

    pl.semaphore_wait(barrier, 2 + (experts - 1) + 2 * experts)
    for i in range(3):
        for copy in (local[3:4], local[4:5], local[5:])[i]:
            copy.wait()
        each(lambda c: weight_copy(i, c).start())

    def slots_of(route):
        onehot = (iota((SLOTS, tok), 0) == route).astype(F32)
        earlier = (iota((tok, tok), 0) < iota((tok, tok), 1)).astype(F32).astype(BF16)
        before = dot(onehot.astype(BF16), earlier)
        place = jnp.sum(before * onehot, axis=0, keepdims=True)
        return route.astype(F32) * SLOTS, place

    def chosen(first, place, q):
        if q < 0:
            slot = jnp.where(place < SLOTS, first + place, -1.0)
        else:
            slot = jnp.where(place >= SLOTS, first + (place - SLOTS) + q * EXTRA, -1.0)
        return (slot == iota((main, tok), 0).astype(F32)).astype(F32)

    for o in range(2):
        first, place = slots_of((fwd_route, bwd_route)[o][...])
        for q in range(1 + EXTRA):
            sel_in[o, q] = chosen(first, place, q - 1).astype(BF16)

    for o in range(2):
        message(1, o).start()
        message(2, o).start()

    for i in range(3):
        o = min(i, 1)
        local[i].wait()

        def pack(c, i=i, o=o):
            rows = rows_in[i, :, cols(c)]
            packed[i, c, :, 0:part] = dot(sel_in[o, 0], rows).astype(BF16)
            total = dot(sel_in[o, 1], rows[:, 0:quarter])
            for q in range(1, EXTRA):
                total += dot(sel_in[o, 1 + q], rows[:, q * quarter : (q + 1) * quarter])
            packed[i, c, :, part:] = total.astype(BF16)
            for k in range(1, experts):
                dispatch(i, c, k).start()
            tokens[i, set_of(me), c, slot_rows(place_of(me))] = packed[i, c, slot_rows(me)]

        each(pack)

    for o in range(2):
        message(0, o).start()

    def pass_on(i, s, c):
        for place in range(members):
            j = source(s, place)

            @pl.when(j != me)
            def _():
                dispatch_from(i, c, j).wait_recv()

        mate_copy(i, s, c).start()

    for i in range(3):
        each(lambda c: pass_on(i, 0, c))

    extra = members * EXTRA
    for q in range(EXTRA):
        r = iota((2 * extra, 2 * block), 0)
        i = iota((2 * extra, 2 * block), 1)
        unfold[q] = (i == (r // EXTRA) * SLOTS + q * EXTRA + r % EXTRA).astype(F32).astype(BF16)
        r = iota((2 * block, 2 * extra), 1)
        i = iota((2 * block, 2 * extra), 0)
        fold[q] = (i == (r // EXTRA) * SLOTS + q * EXTRA + r % EXTRA).astype(F32).astype(BF16)

    for o in range(2):
        message(1, o).wait_recv()
        message(2, o).wait_recv()
        first, place = slots_of(far_route[o])
        whole = chosen(first, place, -1).T.astype(BF16)
        for q in range(EXTRA):
            sel_out[o, q, :, 0:main] = whole
            sel_out[o, q, :, main : 2 * main] = chosen(first, place, q).T.astype(BF16)
        prob[o] = jnp.broadcast_to(far_prob[o], (tok, tok)).T

    def load(i, s, c):
        stack[0 : 2 * block] = tokens[i, s, c, :, 0:part]
        folded = tokens[i, s, c, :, part:]
        for q in range(EXTRA):
            stack[2 * block :, q * quarter : (q + 1) * quarter] = dot(unfold[q], folded).astype(BF16)

    def store(o, s, c, value):
        mine[o, s, c, :, 0:part] = value[0:block].astype(BF16)
        theirs[o, s, c, :, 0:part] = value[block : 2 * block].astype(BF16)
        rest = value[2 * block :].astype(BF16)
        total = dot(fold[0], rest[:, 0:quarter])
        for q in range(1, EXTRA):
            total += dot(fold[q], rest[:, q * quarter : (q + 1) * quarter])
        mine[o, s, c, :, part:] = total[0:block].astype(BF16)
        theirs[o, s, c, :, part:] = total[block:].astype(BF16)
        result_copy(o, s, c).start()

    def project(i, s, c):
        load(i, s, c)
        for half in range(2):
            at = pl.ds(half * hdev, hdev)
            acc[2 * i, :, at] += dot(stack[...], gate[half, cols(c)])
            acc[2 * i + 1, :, at] += dot(stack[...], up[half, cols(c)])

    def first_part(s):
        acc[...] = jnp.zeros_like(acc)

        def forward_in_step(c):
            mate_copy(0, s, c).wait_recv()
            if s == 0:
                weight_copy(0, c).wait_recv()
                weight_copy(1, c).wait_recv()
            project(0, s, c)

        def backward_in_step(c):
            mate_copy(1, s, c).wait_recv()
            project(1, s, c)

        def down_step(c):
            if s == 0:
                weight_copy(2, c).wait_recv()
            store(0, s, c, dot(hidden[...], down[c]))

        def cot_step(c):
            mate_copy(2, s, c).wait_recv()
            load(2, s, c)
            acc[4] += dot_last(stack[...], down[c])

        def both_steps(c):
            down_step(c)
            cot_step(c)

        each(forward_in_step)
        gate_pre = acc[0]
        hidden[...] = (gate_pre / (1.0 + jnp.exp(-gate_pre)) * acc[1]).astype(BF16)
        if s == 0:
            each(backward_in_step)
            each(both_steps)
        else:
            each(down_step)
            each(backward_in_step)
            each(cot_step)

    def second_part(s, beside):
        back_gate = acc[2]
        back_hid = acc[4]
        g = 1.0 / (1.0 + jnp.exp(-back_gate))
        grads[0] = (back_hid * acc[3] * g * (1.0 + back_gate * (1.0 - g))).astype(BF16)
        grads[1] = (back_hid * back_gate * g).astype(BF16)

        def backward_step(c):
            total = dot_last(grads[0, :, 0:hdev], gate[0, cols(c)])
            total += dot_last(grads[0, :, hdev:], gate[1, cols(c)])
            total += dot_last(grads[1, :, 0:hdev], up[0, cols(c)])
            total += dot_last(grads[1, :, hdev:], up[1, cols(c)])
            store(1, s, c, total)
            beside(c)

        each(backward_step)

    def return_step(o, s, c):
        result_copy(o, s, c).wait_recv()
        summed[o, s, c] = (mine[o, s, c].astype(F32) + others[o, s, c].astype(F32)).astype(BF16)
        for place in range(members):
            give(o, s, c, place).start()

    def finish(o, c):
        for j in range(experts):
            give_from(o, c, j).wait_recv()
        scale = jnp.concatenate([prob[o]] * (quarter // tok), axis=1)
        for q in range(EXTRA):
            at = pl.ds(multiple(c * part + q * quarter, quarter), quarter)
            branch = dot(sel_out[o, q, :, 0:main], back[o, c, :, q * quarter : (q + 1) * quarter])
            branch += dot(sel_out[o, q, :, main:], back[o, c, :, part:])
            value = resid[o, :, at].astype(F32) + scale * branch
            final[o, c, :, q * quarter : (q + 1) * quarter] = value.astype(BF16)
        out_copy(o, c).start()

    for s in range(SETS):
        first_part(s)
        if s + 1 < SETS:
            each(lambda c: pass_on(0, s + 1, c))
            second_part(s, lambda c: None)
            for i in range(1, 3):
                each(lambda c: pass_on(i, s + 1, c))
            each(lambda c: return_step(0, s, c))
            each(lambda c: return_step(1, s, c))
        else:
            second_part(s, lambda c: return_step(0, s, c))
            each(lambda c: return_step(1, s, c))

    for o in range(2):
        message(0, o).wait_recv()
    each(lambda c: finish(0, c))
    each(lambda c: finish(1, c))

    def drain(c):
        for i in range(3):
            weight_copy(i, c).wait_send()
            for s in range(SETS):
                mate_copy(i, s, c).wait_send()
            for k in range(1, experts):
                dispatch(i, c, k).wait_send()
        for o in range(2):
            for s in range(SETS):
                result_copy(o, s, c).wait_send()
                for place in range(members):
                    give(o, s, c, place).wait_send()
            out_copy(o, c).wait()

    each(drain)
    for i in range(3):
        for o in range(2):
            message(i, o).wait_send()


def on_device(
    forward_in,
    forward_route,
    forward_gate_prob,
    backward_in,
    backward_route,
    backward_gate_prob,
    cotangent,
    w_gate,
    w_up,
    w_down,
):
    experts = lax.axis_size("expert") // GROUP
    pipes = lax.axis_size("pipe")
    _, tok, width = forward_in.shape
    hdev = w_gate.shape[2]
    main = experts * SLOTS
    members = experts // SETS
    block = members * SLOTS
    extra = members * EXTRA
    part = width // CHUNKS
    wide = part + part // EXTRA
    rows = 2 * (block + extra)
    hbm = pl.BlockSpec(memory_space=pl.ANY)
    vmem = pl.BlockSpec(memory_space=pltpu.VMEM)
    dma = pltpu.SemaphoreType.DMA
    return pl.pallas_call(
        functools.partial(kernel, experts, pipes),
        out_shape=[jax.ShapeDtypeStruct(forward_in.shape, BF16)] * 2,
        in_specs=[hbm] * 6 + [vmem] * 4,
        out_specs=[hbm] * 2,
        scratch_shapes=[
            pltpu.VMEM((3, tok, width), BF16),
            pltpu.VMEM((3, CHUNKS, main, wide), BF16),
            pltpu.VMEM((3, SETS, CHUNKS, 2 * block, wide), BF16),
            pltpu.VMEM((2, width, hdev), BF16),
            pltpu.VMEM((2, width, hdev), BF16),
            pltpu.VMEM((CHUNKS, 2 * hdev, part), BF16),
            pltpu.VMEM((rows, part), BF16),
            pltpu.VMEM((5, rows, 2 * hdev), F32),
            pltpu.VMEM((rows, 2 * hdev), BF16),
            pltpu.VMEM((2, rows, 2 * hdev), BF16),
            pltpu.VMEM((2, SETS, CHUNKS, block, wide), BF16),
            pltpu.VMEM((2, SETS, CHUNKS, block, wide), BF16),
            pltpu.VMEM((2, SETS, CHUNKS, block, wide), BF16),
            pltpu.VMEM((2, SETS, CHUNKS, block, wide), BF16),
            pltpu.VMEM((2, CHUNKS, main, wide), BF16),
            pltpu.VMEM((2, tok, width), BF16),
            pltpu.VMEM((2, 1, tok), jnp.int32),
            pltpu.VMEM((2, 1, tok), F32),
            pltpu.VMEM((2, tok, tok), F32),
            pltpu.VMEM((2, CHUNKS, tok, part), BF16),
            pltpu.VMEM((2, 1 + EXTRA, main, tok), BF16),
            pltpu.VMEM((2, EXTRA, tok, 2 * main), BF16),
            pltpu.VMEM((EXTRA, 2 * extra, 2 * block), BF16),
            pltpu.VMEM((EXTRA, 2 * block, 2 * extra), BF16),
            dma((5 + CHUNKS,)),
            dma((3, CHUNKS)),
            dma((3, CHUNKS)),
            dma((3, CHUNKS, experts)),
            dma((3, CHUNKS, experts)),
            dma((3, SETS, CHUNKS)),
            dma((3, SETS, CHUNKS)),
            dma((2, SETS, CHUNKS)),
            dma((2, SETS, CHUNKS)),
            dma((2, CHUNKS, experts)),
            dma((2, CHUNKS, experts)),
            dma((3, 2)),
            dma((3, 2)),
            dma((2, CHUNKS)),
        ],
        compiler_params=pltpu.CompilerParams(
            collective_id=1, has_side_effects=True, vmem_limit_bytes=60 * 2**20
        ),
    )(
        forward_in,
        backward_in,
        cotangent,
        w_gate,
        w_up,
        w_down,
        forward_route.reshape(1, tok),
        backward_route.reshape(1, tok),
        forward_gate_prob.reshape(1, tok),
        backward_gate_prob.reshape(1, tok),
    )


def solution(mesh):
    tokens = P("pipe", "expert", None)
    columns = P("pipe", None, "expert")
    return jax.shard_map(
        lambda *args: tuple(on_device(*args)),
        mesh=mesh,
        in_specs=(tokens,) * 7 + (columns, columns, tokens),
        out_specs=(tokens, tokens),
        check_vma=False,
    )
```

time: 209 us -> 183 us (0.88)
  Pallas kernels: 197 us -> 175 us
  local copies, waits for them, and re-layouts: 8.89 us -> 3.35 us
    pallas_call x1, Pallas kernels: 197 us -> 175 us  [on_device(): pl.pallas_call(functools.partial(kernel, experts, pipes), out_shape=[jax....]
    unnamed x8 -> x4, local copies, waits for them, and re-layouts: 8.89 us -> 3.35 us
where the time goes in v2:
time: 183 us; the launch traced here: 179 us
  Pallas kernels  175 us (96%)
  local copies, waits for them, and re-layouts  3.35 us (2%)
    pallas_call x1, Pallas kernels, on_device(): pl.pallas_call(functools.partial(kernel, experts, pipes), out_shape=[jax....  175 us

profile of v2, /device:TPU:1, one launch (start us, length us, event | category | flops | bytes accessed | tf_op | source)
XLA Modules:
  0.0 179.0 jit_solution(9225563876683984973)
XLA Ops:
  0.6 175.0 %shard_map.113 = (bf16[1,128,4096]{2,1,0:T(8,128)(2,1)}, bf16[1,128,4096]{2,1,0:T(8,128)(2,1)}) custom-call(bf16[1,128,4096]{2,1,0:T(8,128)(2,1)} %fwd_in.1, bf16[1,128,4096]{2,1,0:T(8,128)(2,1)} %bwd_in.1, bf16[1,128,4096]{2,1,0:T(8,128)(2,1)} %cot_in.1, bf16[1,4096,256]{2,1,0:T(8,128)(2,1)} %w_gate.1, bf16[1,4096,256]{2,1,0:T(8,128)(2,1)} %w_up.1, ...), custom_call_target="tpu_custom_call" | custom-call | tf_op jit(solution)/shard_map/pallas_call | solution.py:485
  175.7 0.0 copy-start
  175.7 2.4 %copy.14 = bf16[1,128,4096]{2,1,0:T(8,128)(2,1)} copy(bf16[1,128,4096]{2,1,0:T(8,128)(2,1)} %get-tuple-element.4) | data formatting | bytes 2097152
  178.0 0.0 copy-done
  178.0 1.0 copy.15
Async XLA Ops:
  175.7 2.4 %copy-start = (bf16[1,128,4096]{2,1,0:T(8,128)(2,1)S(1)}, bf16[1,128,4096]{2,1,0:T(8,128)(2,1)}, u32[]{:S(2)}) copy-start(bf16[1,128,4096]{2,1,0:T(8,128)(2,1)} %get-tuple-element.5) | copy-start | bytes 3145732

commit v3 on v2

--- a/solution.py
+++ b/solution.py
@@ -15,7 +15,10 @@
 SLOTS = 16
 EXTRA = 4
 CHUNKS = 4
-SETS = 2
+SPLIT = (8,)
+SETS = len(SPLIT)
+LATE = ((0, 1), (2, 2))
+START = tuple(sum(SPLIT[:s]) for s in range(SETS))
 
 
 def dot(left, right):
@@ -93,8 +96,6 @@
     quarter = part // EXTRA
     hdev = gate.shape[2]
     main = experts * SLOTS
-    members = experts // SETS
-    block = members * SLOTS
 
     section = lax.axis_index("pipe")
     member = lax.axis_index("expert")
@@ -111,15 +112,16 @@
     def peer(k):
         return (me + k) % experts
 
-    def set_of(j):
-        return (j // 4 + j) % SETS
-
-    def place_of(j):
-        return j // SETS
-
-    def source(s, place):
-        z = (place * SETS) // 4
-        return place * SETS + (s + z) % SETS
+    def rank_of(j):
+        z = j // 4
+        return (j + 2 * z + 3) % 4 * 2 + z
+
+    def source(rank):
+        z = rank % 2
+        return z * 4 + (rank // 2 + 1 + 2 * z) % 4
+
+    def own_row(rank):
+        return rank + START[-1] * (rank // SPLIT[0])
 
     def remote(src, dst, send, recv, device):
         return pltpu.make_async_remote_copy(
@@ -146,20 +148,27 @@
             weight_mate,
         )
 
+    def set_rows(s, side=0, count=1):
+        return pl.ds((2 * START[s] + side * SPLIT[s]) * SLOTS, count * SPLIT[s] * SLOTS)
+
+    def part_rows(s):
+        return pl.ds(START[s] * SLOTS, SPLIT[s] * SLOTS)
+
     def dispatch(i, c, k):
         to = peer(k)
         return remote(
             packed.at[i, c, slot_rows(to)],
-            tokens.at[i, set_of(me), c, slot_rows(place_of(me))],
+            tokens.at[i, c, slot_rows(own_row(rank_of(me)))],
             d_send.at[i, c, k],
             d_recv.at[i, c, me],
             (section, to * GROUP + x),
         )
 
-    def dispatch_from(i, c, j):
+    def dispatch_from(i, c, rank):
+        j = source(rank)
         return remote(
             packed.at[i, c, slot_rows(j)],
-            tokens.at[i, set_of(j), c, slot_rows(place_of(j))],
+            tokens.at[i, c, slot_rows(own_row(rank))],
             d_send.at[i, c, 0],
             d_recv.at[i, c, j],
             (section, j * GROUP + x),
@@ -167,8 +176,8 @@
 
     def mate_copy(i, s, c):
         return remote(
-            tokens.at[i, s, c, pl.ds(0, block)],
-            tokens.at[i, s, c, pl.ds(block, block)],
+            tokens.at[i, c, set_rows(s)],
+            tokens.at[i, c, set_rows(s, 1)],
             t_send.at[i, s, c],
             t_recv.at[i, s, c],
             token_mate,
@@ -176,13 +185,17 @@
 
     def result_copy(o, s, c):
         return remote(
-            theirs.at[o, s, c], others.at[o, s, c], c_send.at[o, s, c], c_recv.at[o, s, c], token_mate
-        )
-
-    def give(o, s, c, place):
-        j = source(s, place)
+            theirs.at[o, c, part_rows(s)],
+            others.at[o, c, part_rows(s)],
+            c_send.at[o, s, c],
+            c_recv.at[o, s, c],
+            token_mate,
+        )
+
+    def give(o, c, rank):
+        j = source(rank)
         return remote(
-            summed.at[o, s, c, slot_rows(place)],
+            summed.at[o, c, slot_rows(rank)],
             back.at[o, c, slot_rows(me)],
             r_send.at[o, c, j],
             r_recv.at[o, c, me],
@@ -191,7 +204,7 @@
 
     def give_from(o, c, j):
         return remote(
-            summed.at[o, 0, c, slot_rows(0)],
+            summed.at[o, c, slot_rows(0)],
             back.at[o, c, slot_rows(j)],
             r_send.at[o, c, j],
             r_recv.at[o, c, j],
@@ -268,46 +281,48 @@
         message(1, o).start()
         message(2, o).start()
 
-    for i in range(3):
-        o = min(i, 1)
-        local[i].wait()
-
-        def pack(c, i=i, o=o):
-            rows = rows_in[i, :, cols(c)]
-            packed[i, c, :, 0:part] = dot(sel_in[o, 0], rows).astype(BF16)
-            total = dot(sel_in[o, 1], rows[:, 0:quarter])
-            for q in range(1, EXTRA):
-                total += dot(sel_in[o, 1 + q], rows[:, q * quarter : (q + 1) * quarter])
-            packed[i, c, :, part:] = total.astype(BF16)
-            for k in range(1, experts):
-                dispatch(i, c, k).start()
-            tokens[i, set_of(me), c, slot_rows(place_of(me))] = packed[i, c, slot_rows(me)]
-
-        each(pack)
+    for copy in local[0:3]:
+        copy.wait()
+
+    def order(k):
+        return (k + 1 - core) % 3
+
+    def pack(n):
+        i, c = order(n // CHUNKS), n % CHUNKS
+        o = (i + 1) // 2
+        rows = rows_in.at[i, :, cols(c)]
+        packed[i, c, :, 0:part] = dot(sel_in[o, 0], rows[...]).astype(BF16)
+        total = dot(sel_in[o, 1], rows[:, 0:quarter])
+        for q in range(1, EXTRA):
+            total += dot(sel_in[o, 1 + q], rows[:, q * quarter : (q + 1) * quarter])
+        packed[i, c, :, part:] = total.astype(BF16)
+        for k in range(1, experts):
+            dispatch(i, c, k).start()
+        tokens[i, c, slot_rows(own_row(rank_of(me)))] = packed[i, c, slot_rows(me)]
+
+    each(pack, 3 * CHUNKS)
 
     for o in range(2):
         message(0, o).start()
 
     def pass_on(i, s, c):
-        for place in range(members):
-            j = source(s, place)
-
-            @pl.when(j != me)
+        for rank in range(START[s], START[s] + SPLIT[s]):
+
+            @pl.when(source(rank) != me)
             def _():
-                dispatch_from(i, c, j).wait_recv()
+                dispatch_from(i, c, rank).wait_recv()
 
         mate_copy(i, s, c).start()
 
-    for i in range(3):
-        each(lambda c: pass_on(i, 0, c))
-
-    extra = members * EXTRA
+    each(lambda n: pass_on(order(n // CHUNKS), 0, n % CHUNKS), CHUNKS * (2 - core))
+
+    most = max(SPLIT)
     for q in range(EXTRA):
-        r = iota((2 * extra, 2 * block), 0)
-        i = iota((2 * extra, 2 * block), 1)
+        r = iota((2 * most * EXTRA, 2 * most * SLOTS), 0)
+        i = iota((2 * most * EXTRA, 2 * most * SLOTS), 1)
         unfold[q] = (i == (r // EXTRA) * SLOTS + q * EXTRA + r % EXTRA).astype(F32).astype(BF16)
-        r = iota((2 * block, 2 * extra), 1)
-        i = iota((2 * block, 2 * extra), 0)
+        r = iota((2 * most * SLOTS, 2 * most * EXTRA), 1)
+        i = iota((2 * most * SLOTS, 2 * most * EXTRA), 0)
         fold[q] = (i == (r // EXTRA) * SLOTS + q * EXTRA + r % EXTRA).astype(F32).astype(BF16)
 
     for o in range(2):
@@ -320,91 +335,84 @@
             sel_out[o, q, :, main : 2 * main] = chosen(first, place, q).T.astype(BF16)
         prob[o] = jnp.broadcast_to(far_prob[o], (tok, tok)).T
 
+    def sizes(s):
+        block = SPLIT[s] * SLOTS
+        extra = SPLIT[s] * EXTRA
+        return block, 2 * extra, 2 * (block + extra)
+
     def load(i, s, c):
-        stack[0 : 2 * block] = tokens[i, s, c, :, 0:part]
-        folded = tokens[i, s, c, :, part:]
+        block, extra, rows = sizes(s)
+        stack[0 : 2 * block] = tokens[i, c, set_rows(s, 0, 2), 0:part]
+        folded = tokens[i, c, set_rows(s, 0, 2), part:]
         for q in range(EXTRA):
-            stack[2 * block :, q * quarter : (q + 1) * quarter] = dot(unfold[q], folded).astype(BF16)
+            stack[2 * block : rows, q * quarter : (q + 1) * quarter] = dot(
+                unfold[q, 0:extra, 0 : 2 * block], folded
+            ).astype(BF16)
+        return stack[0:rows]
 
     def store(o, s, c, value):
-        mine[o, s, c, :, 0:part] = value[0:block].astype(BF16)
-        theirs[o, s, c, :, 0:part] = value[block : 2 * block].astype(BF16)
+        block, extra, rows = sizes(s)
+        at = part_rows(s)
+        mine[o, c, at, 0:part] = value[0:block].astype(BF16)
+        theirs[o, c, at, 0:part] = value[block : 2 * block].astype(BF16)
         rest = value[2 * block :].astype(BF16)
-        total = dot(fold[0], rest[:, 0:quarter])
+        total = dot(fold[0, 0 : 2 * block, 0:extra], rest[:, 0:quarter])
         for q in range(1, EXTRA):
-            total += dot(fold[q], rest[:, q * quarter : (q + 1) * quarter])
-        mine[o, s, c, :, part:] = total[0:block].astype(BF16)
-        theirs[o, s, c, :, part:] = total[block:].astype(BF16)
+            total += dot(fold[q, 0 : 2 * block, 0:extra], rest[:, q * quarter : (q + 1) * quarter])
+        mine[o, c, at, part:] = total[0:block].astype(BF16)
+        theirs[o, c, at, part:] = total[block:].astype(BF16)
         result_copy(o, s, c).start()
 
     def project(i, s, c):
-        load(i, s, c)
+        rows = pl.ds(0, sizes(s)[2])
+        value = load(i, s, c)
         for half in range(2):
             at = pl.ds(half * hdev, hdev)
-            acc[2 * i, :, at] += dot(stack[...], gate[half, cols(c)])
-            acc[2 * i + 1, :, at] += dot(stack[...], up[half, cols(c)])
-
-    def first_part(s):
-        acc[...] = jnp.zeros_like(acc)
-
-        def forward_in_step(c):
-            mate_copy(0, s, c).wait_recv()
-            if s == 0:
-                weight_copy(0, c).wait_recv()
-                weight_copy(1, c).wait_recv()
-            project(0, s, c)
-
-        def backward_in_step(c):
-            mate_copy(1, s, c).wait_recv()
-            project(1, s, c)
-
-        def down_step(c):
-            if s == 0:
-                weight_copy(2, c).wait_recv()
-            store(0, s, c, dot(hidden[...], down[c]))
-
-        def cot_step(c):
-            mate_copy(2, s, c).wait_recv()
-            load(2, s, c)
-            acc[4] += dot_last(stack[...], down[c])
-
-        def both_steps(c):
-            down_step(c)
-            cot_step(c)
-
-        each(forward_in_step)
-        gate_pre = acc[0]
-        hidden[...] = (gate_pre / (1.0 + jnp.exp(-gate_pre)) * acc[1]).astype(BF16)
-        if s == 0:
-            each(backward_in_step)
-            each(both_steps)
-        else:
-            each(down_step)
-            each(backward_in_step)
-            each(cot_step)
-
-    def second_part(s, beside):
-        back_gate = acc[2]
-        back_hid = acc[4]
+            acc[2 * i, rows, at] += dot(value, gate[half, cols(c)])
+            acc[2 * i + 1, rows, at] += dot(value, up[half, cols(c)])
+
+    def forward_in_step(s, c):
+        mate_copy(0, s, c).wait_recv()
+        project(0, s, c)
+
+    def activate(s):
+        rows = pl.ds(0, sizes(s)[2])
+        gate_pre = acc[0, rows]
+        hidden[rows] = (gate_pre / (1.0 + jnp.exp(-gate_pre)) * acc[1, rows]).astype(BF16)
+
+    def backward_in_step(s, c):
+        mate_copy(1, s, c).wait_recv()
+        project(1, s, c)
+
+    def down_step(s, c):
+        store(0, s, c, dot(hidden[pl.ds(0, sizes(s)[2])], down[c]))
+
+    def cot_step(s, c):
+        mate_copy(2, s, c).wait_recv()
+        acc[4, pl.ds(0, sizes(s)[2])] += dot_last(load(2, s, c), down[c])
+
+    def differentiate(s):
+        rows = pl.ds(0, sizes(s)[2])
+        back_gate = acc[2, rows]
+        back_hid = acc[4, rows]
         g = 1.0 / (1.0 + jnp.exp(-back_gate))
-        grads[0] = (back_hid * acc[3] * g * (1.0 + back_gate * (1.0 - g))).astype(BF16)
-        grads[1] = (back_hid * back_gate * g).astype(BF16)
-
-        def backward_step(c):
-            total = dot_last(grads[0, :, 0:hdev], gate[0, cols(c)])
-            total += dot_last(grads[0, :, hdev:], gate[1, cols(c)])
-            total += dot_last(grads[1, :, 0:hdev], up[0, cols(c)])
-            total += dot_last(grads[1, :, hdev:], up[1, cols(c)])
-            store(1, s, c, total)
-            beside(c)
-
-        each(backward_step)
+        grads[0, rows] = (back_hid * acc[3, rows] * g * (1.0 + back_gate * (1.0 - g))).astype(BF16)
+        grads[1, rows] = (back_hid * back_gate * g).astype(BF16)
+
+    def backward_step(s, c):
+        rows = pl.ds(0, sizes(s)[2])
+        total = dot_last(grads[0, rows, 0:hdev], gate[0, cols(c)])
+        total += dot_last(grads[0, rows, hdev:], gate[1, cols(c)])
+        total += dot_last(grads[1, rows, 0:hdev], up[0, cols(c)])
+        total += dot_last(grads[1, rows, hdev:], up[1, cols(c)])
+        store(1, s, c, total)
 
     def return_step(o, s, c):
+        at = part_rows(s)
         result_copy(o, s, c).wait_recv()
-        summed[o, s, c] = (mine[o, s, c].astype(F32) + others[o, s, c].astype(F32)).astype(BF16)
-        for place in range(members):
-            give(o, s, c, place).start()
+        summed[o, c, at] = (mine[o, c, at].astype(F32) + others[o, c, at].astype(F32)).astype(BF16)
+        for rank in range(START[s], START[s] + SPLIT[s]):
+            give(o, c, rank).start()
 
     def finish(o, c):
         for j in range(experts):
@@ -418,23 +426,90 @@
             final[o, c, :, q * quarter : (q + 1) * quarter] = value.astype(BF16)
         out_copy(o, c).start()
 
-    for s in range(SETS):
-        first_part(s)
-        if s + 1 < SETS:
-            each(lambda c: pass_on(0, s + 1, c))
-            second_part(s, lambda c: None)
-            for i in range(1, 3):
-                each(lambda c: pass_on(i, s + 1, c))
-            each(lambda c: return_step(0, s, c))
-            each(lambda c: return_step(1, s, c))
-        else:
-            second_part(s, lambda c: return_step(0, s, c))
-            each(lambda c: return_step(1, s, c))
+    acc[...] = jnp.zeros_like(acc)
+    def follow(c, body):
+        @pl.when(c > 0)
+        def _():
+            body(c - 1)
+
+    def arrived(i, c):
+        weight_copy(i, c).wait_recv()
+
+    def late_tokens(first, last):
+        each(lambda n: pass_on(first + n // CHUNKS, 0, n % CHUNKS), CHUNKS * (last - first))
+
+    def forward(first):
+        def into(c):
+            if first:
+                arrived(0, c)
+                arrived(1, c)
+            forward_in_step(0, c)
+
+        def out(c):
+            if first:
+                arrived(2, c)
+                for at, i in LATE:
+
+                    @pl.when(c == at)
+                    def _():
+                        late_tokens(i, i + 1)
+
+            down_step(0, c)
+            follow(c, lambda before: return_step(0, 0, before))
+
+        each(into)
+        activate(0)
+        each(out)
+
+    def backward(first):
+        def into(c):
+            if first:
+                arrived(0, c)
+                arrived(1, c)
+            backward_in_step(0, c)
+
+        def against(c):
+            if first:
+                arrived(2, c)
+            cot_step(0, c)
+
+        def out(c):
+            backward_step(0, c)
+            follow(c, lambda before: return_step(1, 0, before))
+
+        each(into)
+        each(against)
+        if first:
+            late_tokens(0, 1)
+        differentiate(0)
+        each(out)
+
+    @pl.when(core == 1)
+    def _():
+        forward(True)
+        return_step(0, 0, CHUNKS - 1)
+        backward(False)
+        return_step(1, 0, CHUNKS - 1)
+
+    @pl.when(core == 0)
+    def _():
+        backward(True)
+        return_step(1, 0, CHUNKS - 1)
+        forward(False)
+        return_step(0, 0, CHUNKS - 1)
 
     for o in range(2):
         message(0, o).wait_recv()
-    each(lambda c: finish(0, c))
-    each(lambda c: finish(1, c))
+
+    @pl.when(core == 0)
+    def _():
+        each(lambda c: finish(0, c))
+        each(lambda c: finish(1, c))
+
+    @pl.when(core == 1)
+    def _():
+        each(lambda c: finish(1, c))
+        each(lambda c: finish(0, c))
 
     def drain(c):
         for i in range(3):
@@ -446,8 +521,8 @@
         for o in range(2):
             for s in range(SETS):
                 result_copy(o, s, c).wait_send()
-                for place in range(members):
-                    give(o, s, c, place).wait_send()
+            for rank in range(experts):
+                give(o, c, rank).wait_send()
             out_copy(o, c).wait()
 
     each(drain)
@@ -473,9 +548,8 @@
     _, tok, width = forward_in.shape
     hdev = w_gate.shape[2]
     main = experts * SLOTS
-    members = experts // SETS
-    block = members * SLOTS
-    extra = members * EXTRA
+    block = max(SPLIT) * SLOTS
+    extra = max(SPLIT) * EXTRA
     part = width // CHUNKS
     wide = part + part // EXTRA
     rows = 2 * (block + extra)
@@ -490,7 +564,7 @@
         scratch_shapes=[
             pltpu.VMEM((3, tok, width), BF16),
             pltpu.VMEM((3, CHUNKS, main, wide), BF16),
-            pltpu.VMEM((3, SETS, CHUNKS, 2 * block, wide), BF16),
+            pltpu.VMEM((3, CHUNKS, 2 * main, wide), BF16),
             pltpu.VMEM((2, width, hdev), BF16),
             pltpu.VMEM((2, width, hdev), BF16),
             pltpu.VMEM((CHUNKS, 2 * hdev, part), BF16),
@@ -498,10 +572,10 @@
             pltpu.VMEM((5, rows, 2 * hdev), F32),
             pltpu.VMEM((rows, 2 * hdev), BF16),
             pltpu.VMEM((2, rows, 2 * hdev), BF16),
-            pltpu.VMEM((2, SETS, CHUNKS, block, wide), BF16),
-            pltpu.VMEM((2, SETS, CHUNKS, block, wide), BF16),
-            pltpu.VMEM((2, SETS, CHUNKS, block, wide), BF16),
-            pltpu.VMEM((2, SETS, CHUNKS, block, wide), BF16),
+            pltpu.VMEM((2, CHUNKS, main, wide), BF16),
+            pltpu.VMEM((2, CHUNKS, main, wide), BF16),
+            pltpu.VMEM((2, CHUNKS, main, wide), BF16),
+            pltpu.VMEM((2, CHUNKS, main, wide), BF16),
             pltpu.VMEM((2, CHUNKS, main, wide), BF16),
             pltpu.VMEM((2, tok, width), BF16),
             pltpu.VMEM((2, 1, tok), jnp.int32),

time: 183 us -> 179 us (0.978); the launches traced: 179 us -> 178 us
  no operation moved by 1% of the time
where the time goes in v3:
time: 179 us; the launch traced here: 178 us
  Pallas kernels  174 us (97%)
  local copies, waits for them, and re-layouts  3.35 us (2%)
    pallas_call x1, Pallas kernels, on_device(): pl.pallas_call(functools.partial(kernel, experts, pipes), out_shape=[jax....  174 us

profile of v3, /device:TPU:1, one launch (start us, length us, event | category | flops | bytes accessed | tf_op | source)
XLA Modules:
  0.0 178.5 jit_solution(15986785005436225167)
XLA Ops:
  0.6 174.5 %shard_map.113 = (bf16[1,128,4096]{2,1,0:T(8,128)(2,1)}, bf16[1,128,4096]{2,1,0:T(8,128)(2,1)}) custom-call(bf16[1,128,4096]{2,1,0:T(8,128)(2,1)} %fwd_in.1, bf16[1,128,4096]{2,1,0:T(8,128)(2,1)} %bwd_in.1, bf16[1,128,4096]{2,1,0:T(8,128)(2,1)} %cot_in.1, bf16[1,4096,256]{2,1,0:T(8,128)(2,1)} %w_gate.1, bf16[1,4096,256]{2,1,0:T(8,128)(2,1)} %w_up.1, ...), custom_call_target="tpu_custom_call" | custom-call | tf_op jit(solution)/shard_map/pallas_call | solution.py:559
  175.1 0.0 copy-start
  175.1 2.4 %copy.14 = bf16[1,128,4096]{2,1,0:T(8,128)(2,1)} copy(bf16[1,128,4096]{2,1,0:T(8,128)(2,1)} %get-tuple-element.4) | data formatting | bytes 2097152
  177.5 0.0 copy-done
  177.5 1.0 copy.15
Async XLA Ops:
  175.1 2.4 %copy-start = (bf16[1,128,4096]{2,1,0:T(8,128)(2,1)S(1)}, bf16[1,128,4096]{2,1,0:T(8,128)(2,1)}, u32[]{:S(2)}) copy-start(bf16[1,128,4096]{2,1,0:T(8,128)(2,1)} %get-tuple-element.5) | copy-start | bytes 3145732

commit v4 on v3

--- a/solution.py
+++ b/solution.py
@@ -471,6 +471,11 @@
         def against(c):
             if first:
                 arrived(2, c)
+
+                @pl.when(c == CHUNKS - 1)
+                def _():
+                    late_tokens(0, 1)
+
             cot_step(0, c)
 
         def out(c):
@@ -479,8 +484,6 @@
 
         each(into)
         each(against)
-        if first:
-            late_tokens(0, 1)
         differentiate(0)
         each(out)
 

time: 179 us -> 179 us (level)
  no operation moved by 1% of the time
where the time goes in v4:
time: 179 us; the launch traced here: 178 us
  Pallas kernels  174 us (97%)
  local copies, waits for them, and re-layouts  3.35 us (2%)
    pallas_call x1, Pallas kernels, on_device(): pl.pallas_call(functools.partial(kernel, experts, pipes), out_shape=[jax....  174 us

profile of v4, /device:TPU:1, one launch (start us, length us, event | category | flops | bytes accessed | tf_op | source)
XLA Modules:
  0.0 178.5 jit_solution(352481281969435872)
XLA Ops:
  0.6 174.5 %shard_map.113 = (bf16[1,128,4096]{2,1,0:T(8,128)(2,1)}, bf16[1,128,4096]{2,1,0:T(8,128)(2,1)}) custom-call(bf16[1,128,4096]{2,1,0:T(8,128)(2,1)} %fwd_in.1, bf16[1,128,4096]{2,1,0:T(8,128)(2,1)} %bwd_in.1, bf16[1,128,4096]{2,1,0:T(8,128)(2,1)} %cot_in.1, bf16[1,4096,256]{2,1,0:T(8,128)(2,1)} %w_gate.1, bf16[1,4096,256]{2,1,0:T(8,128)(2,1)} %w_up.1, ...), custom_call_target="tpu_custom_call" | custom-call | tf_op jit(solution)/shard_map/pallas_call | solution.py:562
  175.1 0.0 copy-start
  175.1 2.4 %copy.14 = bf16[1,128,4096]{2,1,0:T(8,128)(2,1)} copy(bf16[1,128,4096]{2,1,0:T(8,128)(2,1)} %get-tuple-element.4) | data formatting | bytes 2097152
  177.5 0.0 copy-done
  177.5 1.0 copy.15
Async XLA Ops:
  175.1 2.4 %copy-start = (bf16[1,128,4096]{2,1,0:T(8,128)(2,1)S(1)}, bf16[1,128,4096]{2,1,0:T(8,128)(2,1)}, u32[]{:S(2)}) copy-start(bf16[1,128,4096]{2,1,0:T(8,128)(2,1)} %get-tuple-element.5) | copy-start | bytes 3145732
